TPU v7x, 32 devices: a whole 2x2x4 slice. The times are simulated.
32 devices in a mesh: blk: 8 (over z, y), lag: 4 (over x, core).
Axes of the slice: x: 2, y: 2, z: 4, core: 2. Of those that a mesh axis runs over, the one named last changes fastest.
Arguments:
- seismograms: float32 [1024, 3, 1024], P(('blk', 'lag')), may hold values from -70 to 70
- onset_shift: int32 [1024], P(('blk', 'lag')), may hold values from 0 to 63
- start_bits: int32 [1024], P(('blk', 'lag')), may hold values from 0 to 65535
Outputs:
- embedding: float32 [16, 1024], P(None, ('blk', 'lag'))
Inputs may be any that keep to these rules, and one draw needn't show every extreme that they name: `start_bits`: bit k of an event's code is its entry in starting vector k.
All inputs are finite; a program needn't handle non-finite values.
Results may differ from a plain program's by a relative error of at most 0.0077.
Values may be sent and summed in bfloat16 or wider, within the bound.
A program may use at most 64 MiB of HBM per device.

v0:
```python
import jax
import jax.numpy as jnp
from jax import lax
from jax.sharding import PartitionSpec as P

SAMPLES = 1024
MAXLAG = 64
LAGS = 65
OFFMAX = 64
VECTORS = 16
ITERS = 3
sharpness = 64.0


def passed_along(value, axis, steps):
    count = lax.axis_size(axis)
    pairs = [(source, (source + steps) % count) for source in range(count)]
    return lax.ppermute(value, axis, pairs)


def align_unit(seismograms, onset_shift):
    padded = jnp.pad(seismograms, ((0, 0), (0, 0), (0, OFFMAX)))

    def slide(record, offset_at):
        return lax.dynamic_slice_in_dim(record, offset_at, SAMPLES, 1)

    aligned = jax.vmap(slide)(padded, onset_shift)
    energy = jnp.sum(aligned * aligned, axis=(1, 2))
    return (aligned * lax.rsqrt(energy + 1e-06)[:, None, None]).astype(jnp.bfloat16)


def neighbour_waves(unit_waves):
    centre = lax.all_gather(unit_waves, "lag", axis=0, tiled=True)
    beyond = passed_along(centre, "blk", -1)
    before = passed_along(centre, "blk", 1)
    blocks = (before, centre, beyond)
    return blocks


def neighbour_vectors(scaled):
    centre = lax.all_gather(scaled, "lag", axis=1, tiled=True)
    before = passed_along(centre, "blk", 1)
    beyond = passed_along(centre, "blk", -1)
    return jnp.concatenate((before, centre, beyond), 1)


def band_affinity(unit_waves, blocks):
    own_count = unit_waves.shape[0]
    flat_width = unit_waves.shape[1] * unit_waves.shape[2]
    padded = jnp.pad(unit_waves, ((0, 0), (0, 0), (MAXLAG, MAXLAG)))
    lag_group = 5
    flattened = [block.reshape(block.shape[0], flat_width) for block in blocks]

    def one_group(runnings, first_lag):
        shifted = jnp.concatenate(
            [
                lax.dynamic_slice_in_dim(
                    padded, 2 * MAXLAG - 2 * (first_lag + offset), SAMPLES, 2
                ).reshape(own_count, flat_width)
                for offset in range(lag_group)
            ],
            0,
        )
        updated = []
        for running, columns in zip(runnings, flattened):
            scores = lax.dot_general(
                shifted, columns, (((1,), (1,)), ((), ())), preferred_element_type=jnp.float32
            )
            weights = jnp.exp(sharpness * scores).reshape(lag_group, own_count, columns.shape[0])
            updated.append(running + jnp.sum(weights, axis=0))
        return (tuple(updated), None)

    starting = tuple(
        (jnp.zeros((own_count, columns.shape[0]), jnp.float32) for columns in flattened)
    )
    runnings, unused = lax.scan(
        one_group, starting, jnp.arange(0, LAGS, lag_group, dtype=jnp.int32)
    )
    return jnp.concatenate(runnings, 1)


def local(seismograms, onset_shift, start_bits):
    own_count = seismograms.shape[0]
    highest = lax.Precision.HIGHEST
    unit_waves = align_unit(seismograms, onset_shift)
    blocks = neighbour_waves(unit_waves)
    affinity = band_affinity(unit_waves, blocks)
    block_length = affinity.shape[1] // 3
    member = lax.axis_index("lag")
    column_ids = jnp.arange(3 * block_length, dtype=jnp.int32)
    self_ids = block_length + member * own_count + jnp.arange(own_count, dtype=jnp.int32)
    affinity = jnp.where(
        column_ids[None, :] == self_ids[:, None], jnp.zeros_like(affinity), affinity
    )
    degree = jnp.sum(affinity, axis=1)
    root_degree = jnp.sqrt(degree)
    inverse = lax.rsqrt(degree)
    events_all = own_count * lax.axis_size("blk") * lax.axis_size("lag")
    powers = 2 ** jnp.arange(VECTORS, dtype=jnp.int32)
    vectors = (start_bits[None, :] // powers[:, None] % 2).astype(jnp.float32)
    degree_total, projection = lax.psum(
        (jnp.sum(degree), jnp.dot(vectors, root_degree, precision=highest)), ("blk", "lag")
    )
    for iteration in range(ITERS):
        neighbours = neighbour_vectors(vectors * inverse)
        applied = lax.dot_general(neighbours, affinity, (((1,), (1,)), ((), ())), precision=highest)
        deflated = applied * inverse - root_degree * (projection / degree_total)[:, None]
        gram_local = jnp.dot(deflated, deflated.T, precision=highest)
        carried_local = jnp.dot(deflated, root_degree, precision=highest)
        gram_sum, carried = lax.psum((gram_local, carried_local), ("blk", "lag"))
        factor = jnp.linalg.cholesky(gram_sum / events_all)
        vectors = lax.linalg.triangular_solve(factor, deflated, left_side=True, lower=True)
        projection = lax.linalg.triangular_solve(
            factor, carried[:, None], left_side=True, lower=True
        )[:, 0]
    return vectors


def solution(mesh):
    return jax.shard_map(
        local,
        mesh=mesh,
        in_specs=(P(("blk", "lag"), None, None), P(("blk", "lag")), P(("blk", "lag"))),
        out_specs=P(None, ("blk", "lag")),
        check_vma=False,
    )
```

profile of v0, /device:TPU:10, one launch (start us, length us, event | category | flops | bytes accessed | tf_op | source)
XLA Modules:
  0.0 432.6 jit_solution(3291205660569676358)
XLA Ops:
  2.1 64.4 %while.19 = (s32[]{:T(128)}, f32[32,3,1088]{2,1,0:T(4,128)S(1)}, s32[32,3]{0,1:T(4,128)S(1)}, f32[32,3,1024]{2,1,0:T(4,128)S(1)}, s32[]{:T(128)}) while((s32[]{:T(128)}, f32[32,3,1088]{2,1,0:T(4,128)S(1)}, s32[32,3]{0,1:T(4,128)S(1)}, f32[32,3,1024]{2,1,0:T(4,128)S(1)}, s32[]{:T(128)}) %tuple.64), condition=%wide.while_cond, body=%wide.while_body.sunk | while | flops 2 | bytes 32893 | solution.py:25
  2.8 1.3 dynamic-slice_dynamic-update-slice_fusion.2
  4.8 1.3 dynamic-slice_dynamic-update-slice_fusion.2
  6.8 1.3 dynamic-slice_dynamic-update-slice_fusion.2
  8.8 1.3 dynamic-slice_dynamic-update-slice_fusion.2
  10.8 1.3 dynamic-slice_dynamic-update-slice_fusion.2
  12.8 1.3 dynamic-slice_dynamic-update-slice_fusion.2
  14.8 1.3 dynamic-slice_dynamic-update-slice_fusion.2
  16.8 1.3 dynamic-slice_dynamic-update-slice_fusion.2
  18.9 1.3 dynamic-slice_dynamic-update-slice_fusion.2
  20.9 1.3 dynamic-slice_dynamic-update-slice_fusion.2
  22.9 1.3 dynamic-slice_dynamic-update-slice_fusion.2
  24.9 1.3 dynamic-slice_dynamic-update-slice_fusion.2
  26.9 1.3 dynamic-slice_dynamic-update-slice_fusion.2
  28.9 1.3 dynamic-slice_dynamic-update-slice_fusion.2
  30.9 1.3 dynamic-slice_dynamic-update-slice_fusion.2
  32.9 1.3 dynamic-slice_dynamic-update-slice_fusion.2
  35.0 1.3 dynamic-slice_dynamic-update-slice_fusion.2
  37.0 1.3 dynamic-slice_dynamic-update-slice_fusion.2
  39.0 1.3 dynamic-slice_dynamic-update-slice_fusion.2
  41.0 1.3 dynamic-slice_dynamic-update-slice_fusion.2
  43.0 1.3 dynamic-slice_dynamic-update-slice_fusion.2
  45.0 1.3 dynamic-slice_dynamic-update-slice_fusion.2
  47.0 1.3 dynamic-slice_dynamic-update-slice_fusion.2
  49.0 1.3 dynamic-slice_dynamic-update-slice_fusion.2
  51.1 1.3 dynamic-slice_dynamic-update-slice_fusion.2
  53.1 1.3 dynamic-slice_dynamic-update-slice_fusion.2
  55.1 1.3 dynamic-slice_dynamic-update-slice_fusion.2
  57.1 1.3 dynamic-slice_dynamic-update-slice_fusion.2
  59.1 1.3 dynamic-slice_dynamic-update-slice_fusion.2
  61.1 1.3 dynamic-slice_dynamic-update-slice_fusion.2
  63.1 1.3 dynamic-slice_dynamic-update-slice_fusion.2
  65.1 1.3 dynamic-slice_dynamic-update-slice_fusion.2
  67.1 8.2 %all_gather.12 = bf16[128,3,1024]{2,0,1:T(8,128)(2,1)S(1)} all-gather(bf16[32,3,1024]{2,0,1:T(8,128)(2,1)S(1)} %fusion.12), channel_id=1, replica_groups=mesh['blk'=8,'lag'=4] {'lag'}, dimensions={0}, use_global_device_ids=true | all-gather | bytes 983040 | tf_op jit(solution)/shard_map/all_gather | solution.py:33
  75.6 1.5 collective-permute-start.1
  79.1 33.3 %collective-permute-done.1 = bf16[128,3,1024]{0,2,1:T(8,128)(2,1)} collective-permute-done((bf16[128,3,1024]{0,2,1:T(8,128)(2,1)S(1)}, bf16[128,3,1024]{0,2,1:T(8,128)(2,1)}, u32[]{:S(2)}, u32[]{:S(2)}) %collective-permute-start.1) | collective-permute-done | bytes 786464 | tf_op jit(solution)/shard_map/ppermute | solution.py:18
  112.4 1.4 copy.34
  115.0 103.0 %while.20 = (s32[]{:T(128)}, f32[32,128]{1,0:T(8,128)S(1)}, f32[32,128]{1,0:T(8,128)S(1)}, f32[32,128]{1,0:T(8,128)S(1)}, s32[13]{0:T(128)S(1)}, /*index=5*/bf16...) while((s32[]{:T(128)}, f32[32,128]{1,0:T(8,128)S(1)}, ...), condition=%wide.region_5.6_spmd.clone, body=%wide.region_1.5_spmd.clone.sunk | while | flops 377622560 | bytes 15041106 | solution.py:76
  118.9 1.4 constant_dynamic-slice_fusion.9
  126.8 1.4 constant_dynamic-slice_fusion.9
  134.7 1.4 constant_dynamic-slice_fusion.9
  142.6 1.4 constant_dynamic-slice_fusion.9
  150.6 1.4 constant_dynamic-slice_fusion.9
  158.5 1.4 constant_dynamic-slice_fusion.9
  166.4 1.4 constant_dynamic-slice_fusion.9
  174.3 1.4 constant_dynamic-slice_fusion.9
  182.3 1.4 constant_dynamic-slice_fusion.9
  190.2 1.4 constant_dynamic-slice_fusion.9
  198.1 1.4 constant_dynamic-slice_fusion.9
  206.0 1.4 constant_dynamic-slice_fusion.9
  214.0 1.4 constant_dynamic-slice_fusion.9
  219.3 5.2 %all-gather = f32[4,32,16]{1,2,0:T(8,128)S(1)} all-gather(f32[1,32,16]{1,2,0:T(8,128)S(1)} %multiply_bitcast_fusion), channel_id=1, replica_groups=mesh['blk'=8,'lag'=4] {'lag'}, dimensions={0}, use_global_device_ids=true | all-gather | bytes 10240 | tf_op jit(solution)/shard_map/all_gather | solution.py:41
  226.6 42.9 %all-reduce.5 = (f32[16]{0:T(128)S(1)}, f32[]{:T(128)}) all-reduce(f32[16]{0:T(128)S(1)} %convolution_bitcast_fusion.4, f32[]{:T(128)} %get-tuple-element.209), channel_id=1, replica_groups=mesh['blk'=8,'lag'=4] {'blk','lag'}, use_global_device_ids=true, to_apply=%region_7.8 | all-reduce | flops 17 | bytes 136 | tf_op jit(solution)/shard_map/psum | solution.py:101
  270.7 39.1 %all-reduce.4 = (f32[16,16]{0,1:T(8,128)S(1)}, f32[16,1]{0,1:T(1,128)S(1)}) all-reduce(f32[16,16]{0,1:T(8,128)S(1)} %fusion.69, f32[16,1]{0,1:T(1,128)S(1)} %convolution_bitcast_fusion.3), channel_id=1, replica_groups=mesh['blk'=8,'lag'=4] {'blk','lag'}, use_global_device_ids=true, to_apply=%region_10.11 | all-reduce | flops 272 | bytes 2176 | tf_op jit(solution)/shard_map/psum | solution.py:110
  309.9 1.5 cholesky.59
  314.2 5.2 %all-gather.1 = f32[4,32,16]{1,2,0:T(8,128)S(1)} all-gather(f32[1,32,16]{1,2,0:T(8,128)S(1)} %fusion.6), channel_id=1, replica_groups=mesh['blk'=8,'lag'=4] {'lag'}, dimensions={0}, use_global_device_ids=true | all-gather | bytes 10240 | tf_op jit(solution)/shard_map/all_gather | solution.py:41
  319.5 2.7 collective-permute-start.5
  323.6 3.2 collective-permute-done.4
  327.3 43.0 %all-reduce.3 = (f32[16,16]{0,1:T(8,128)S(1)}, f32[16,1]{0,1:T(1,128)S(1)}) all-reduce(f32[16,16]{0,1:T(8,128)S(1)} %fusion.70, f32[16,1]{0,1:T(1,128)S(1)} %convolution_bitcast_fusion.1), channel_id=1, replica_groups=mesh['blk'=8,'lag'=4] {'blk','lag'}, use_global_device_ids=true, to_apply=%region_14.18 | all-reduce | flops 272 | bytes 2176 | tf_op jit(solution)/shard_map/psum | solution.py:110
  370.4 1.5 cholesky.70
  374.7 5.2 %all-gather.2 = f32[4,32,16]{1,2,0:T(8,128)S(1)} all-gather(f32[1,32,16]{1,2,0:T(8,128)S(1)} %fusion.4), channel_id=1, replica_groups=mesh['blk'=8,'lag'=4] {'lag'}, dimensions={0}, use_global_device_ids=true | all-gather | bytes 10240 | tf_op jit(solution)/shard_map/all_gather | solution.py:41
  380.0 2.0 collective-permute-start.6
  385.0 42.7 %psum.55 = f32[16,16]{0,1:T(8,128)S(1)} all-reduce(f32[16,16]{0,1:T(8,128)S(1)} %fusion.71), channel_id=1, replica_groups=mesh['blk'=8,'lag'=4] {'blk','lag'}, use_global_device_ids=true, to_apply=%region_16.20 | all-reduce | flops 256 | bytes 2048 | tf_op jit(solution)/shard_map/psum | solution.py:110
  427.7 1.5 cholesky.81
  (418 shorter events, 87.6 us)
Async XLA Ops:
  0.0 0.7 copy-start.2
  75.6 36.8 %collective-permute-start.1 = (bf16[128,3,1024]{0,2,1:T(8,128)(2,1)S(1)}, bf16[128,3,1024]{0,2,1:T(8,128)(2,1)}, u32[]{:S(2)}, u32[]{:S(2)}) collective-permute-start(bf16[128,3,1024]{0,2,1:T(8,128)(2,1)S(1)} %copy.28), channel_id=1, source_target_pairs={{0,28},{4,0},{8,4},{12,8},{16,12},{20,16},{24,20},{28,24},{1,29},{... | collective-permute-start | bytes 2359304 | tf_op jit(solution)/shard_map/ppermute | solution.py:18
  77.1 36.8 %collective-permute-start = (bf16[128,3,1024]{0,2,1:T(8,128)(2,1)S(1)}, bf16[128,3,1024]{0,2,1:T(8,128)(2,1)S(1)}, u32[]{:S(2)}, u32[]{:S(2)}) collective-permute-start(bf16[128,3,1024]{0,2,1:T(8,128)(2,1)S(1)} %copy.28), channel_id=1, source_target_pairs={{0,4},{4,8},{8,12},{12,16},{16,20},{20,24},{24,28},{28,0},{1,5},{5... | collective-permute-start | bytes 2359304 | tf_op jit(solution)/shard_map/ppermute | solution.py:18
  77.9 0.7 copy-start.1
  121.3 1.1 copy-start
  129.2 1.1 copy-start
  137.2 1.1 copy-start
  145.1 1.1 copy-start
  153.0 1.1 copy-start
  160.9 1.1 copy-start
  168.9 1.1 copy-start
  176.8 1.1 copy-start
  184.7 1.1 copy-start
  192.6 1.1 copy-start
  200.6 1.1 copy-start
  208.5 1.1 copy-start
  216.4 1.1 copy-start
  224.6 45.6 %collective-permute-start.3 = (f32[16,128]{1,0:T(8,128)S(1)}, f32[16,128]{1,0:T(8,128)S(1)}, u32[]{:S(2)}, u32[]{:S(2)}) collective-permute-start(f32[16,128]{1,0:T(8,128)S(1)} %bitcast.222), channel_id=1, source_target_pairs={{0,28},{4,0},{8,4},{12,8},{16,12},{20,16},{24,20},{28,24},{1,29},{... | collective-permute-start | bytes 24584 | tf_op jit(solution)/shard_map/ppermute | solution.py:18
  225.4 44.7 %collective-permute-start.2 = (f32[16,128]{1,0:T(8,128)S(1)}, f32[16,128]{1,0:T(8,128)S(1)}, u32[]{:S(2)}, u32[]{:S(2)}) collective-permute-start(f32[16,128]{1,0:T(8,128)S(1)} %bitcast.223), channel_id=1, source_target_pairs={{0,4},{4,8},{8,12},{12,16},{16,20},{20,24},{24,28},{28,0},{1,5},{5... | collective-permute-start | bytes 24584 | tf_op jit(solution)/shard_map/ppermute | solution.py:18
  319.5 4.1 collective-permute-start.5
  322.2 4.5 %collective-permute-start.4 = (f32[16,128]{1,0:T(8,128)S(1)}, f32[16,128]{1,0:T(8,128)S(1)}, u32[]{:S(2)}, u32[]{:S(2)}) collective-permute-start(f32[16,128]{1,0:T(8,128)S(1)} %bitcast.226), channel_id=1, source_target_pairs={{0,4},{4,8},{8,12},{12,16},{16,20},{20,24},{24,28},{28,0},{1,5},{5... | collective-permute-start | bytes 24584 | tf_op jit(solution)/shard_map/ppermute | solution.py:18
  380.0 3.7 collective-permute-start.7
  380.0 4.6 %collective-permute-start.6 = (f32[16,128]{1,0:T(8,128)S(1)}, f32[16,128]{1,0:T(8,128)S(1)}, u32[]{:S(2)}, u32[]{:S(2)}) collective-permute-start(f32[16,128]{1,0:T(8,128)S(1)} %bitcast.220), channel_id=1, source_target_pairs={{0,4},{4,8},{8,12},{12,16},{16,20},{20,24},{24,28},{28,0},{1,5},{5... | collective-permute-start | bytes 24584 | tf_op jit(solution)/shard_map/ppermute | solution.py:18
where the time goes:
time: 435 us; the launch traced here: 433 us
  blocking collectives  191 us (44%)
  local copies, waits for them, and re-layouts  114 us (26%)
  loops' own time  43.5 us (10%)
  waiting for transfers between devices  38.9 us (9%)
  matrix products  21 us (5%)
  other arithmetic  15.1 us (3%)
  starting transfers between devices  8.82 us (2%)
    psum x3, blocking collectives, local(): gram_sum, carried = lax.psum((gram_local, carried_local), ('blk', 'lag'))  125 us
    gather x96, local copies, waits for them, and re-layouts  64.4 us
    another operation x1, loops' own time, band_affinity(): lax.scan(one_group, starting, jnp.arange(0, LAGS, lag_group, dtype=jnp.in...  43.5 us
    psum x1, blocking collectives, local(): lax.psum((jnp.sum(degree), jnp.dot(vectors, root_degree, precision=highes...  42.9 us
    ppermute x8, waiting for transfers between devices, passed_along(): return lax.ppermute(value, axis, pairs)  38.9 us
    dynamic_slice x13, local copies, waits for them, and re-layouts, one_group(): lax.dynamic_slice_in_dim(padded, 2 * MAXLAG - 2 * (first_lag + offset), S...  18.6 us
    dot_general x39, matrix products, one_group(): lax.dot_general(shifted, columns, (((1,), (1,)), ((), ())), preferred_ele...  16.5 us
    all_gather x3, blocking collectives, neighbour_vectors(): centre = lax.all_gather(scaled, 'lag', axis=1, tiled=True)  15.6 us
  transfers between devices with their start and end apart: 8, of which 5 were waited for; matrix products, arithmetic and copies ran while one was open for 1% of the time, Pallas kernels for 0%

commit v1 on v0

--- a/solution.py
+++ b/solution.py
@@ -10,6 +10,11 @@
 VECTORS = 16
 ITERS = 3
 sharpness = 64.0
+
+
+def axis_by_axis(x, one, other):
+    partial = lax.psum(x, one)
+    return lax.psum(partial, other)
 
 
 def passed_along(value, axis, steps):
@@ -107,7 +112,7 @@
         deflated = applied * inverse - root_degree * (projection / degree_total)[:, None]
         gram_local = jnp.dot(deflated, deflated.T, precision=highest)
         carried_local = jnp.dot(deflated, root_degree, precision=highest)
-        gram_sum, carried = lax.psum((gram_local, carried_local), ("blk", "lag"))
+        gram_sum, carried = axis_by_axis((gram_local, carried_local), "lag", "blk")
         factor = jnp.linalg.cholesky(gram_sum / events_all)
         vectors = lax.linalg.triangular_solve(factor, deflated, left_side=True, lower=True)
         projection = lax.linalg.triangular_solve(

time: 435 us -> 387 us (0.89); the launches traced: 433 us -> 380 us
  blocking collectives: 191 us -> 134 us
    psum x3 -> x6, blocking collectives: 125 us -> 67.1 us  [the longest x3 49.3 us: axis_by_axis(): return lax.psum(partial, other)]
where the time goes in v1:
time: 387 us; the launch traced here: 380 us
  blocking collectives  134 us (35%)
  local copies, waits for them, and re-layouts  114 us (29%)
  loops' own time  43.5 us (11%)
  waiting for transfers between devices  40.9 us (11%)
  matrix products  21 us (5%)
  other arithmetic  15.1 us (4%)
  starting transfers between devices  11.6 us (3%)
    gather x96, local copies, waits for them, and re-layouts  64.4 us
    psum x3, blocking collectives, axis_by_axis(): return lax.psum(partial, other)  49.3 us
    another operation x1, loops' own time, band_affinity(): lax.scan(one_group, starting, jnp.arange(0, LAGS, lag_group, dtype=jnp.in...  43.5 us
    psum x1, blocking collectives, local(): lax.psum((jnp.sum(degree), jnp.dot(vectors, root_degree, precision=highes...  42.9 us
    ppermute x8, waiting for transfers between devices, passed_along(): return lax.ppermute(value, axis, pairs)  40.9 us
    dynamic_slice x13, local copies, waits for them, and re-layouts, one_group(): lax.dynamic_slice_in_dim(padded, 2 * MAXLAG - 2 * (first_lag + offset), S...  18.6 us
    psum x3, blocking collectives, axis_by_axis(): partial = lax.psum(x, one)  17.8 us
    dot_general x39, matrix products, one_group(): lax.dot_general(shifted, columns, (((1,), (1,)), ((), ())), preferred_ele...  16.5 us
  transfers between devices with their start and end apart: 8, of which 5 were waited for; matrix products, arithmetic and copies ran while one was open for 1% of the time, Pallas kernels for 0%

profile of v1, /device:TPU:10, one launch (start us, length us, event | category | flops | bytes accessed | tf_op | source)
XLA Modules:
  0.0 379.8 jit_solution(11786947263786105502)
XLA Ops:
  2.1 64.4 %while.19 = (s32[]{:T(128)}, f32[32,3,1088]{2,1,0:T(4,128)S(1)}, s32[32,3]{0,1:T(4,128)S(1)}, f32[32,3,1024]{2,1,0:T(4,128)S(1)}, s32[]{:T(128)}) while((s32[]{:T(128)}, f32[32,3,1088]{2,1,0:T(4,128)S(1)}, s32[32,3]{0,1:T(4,128)S(1)}, f32[32,3,1024]{2,1,0:T(4,128)S(1)}, s32[]{:T(128)}) %tuple.64), condition=%wide.while_cond, body=%wide.while_body.sunk | while | flops 2 | bytes 32893 | solution.py:30
  2.8 1.3 dynamic-slice_dynamic-update-slice_fusion.2
  4.8 1.3 dynamic-slice_dynamic-update-slice_fusion.2
  6.8 1.3 dynamic-slice_dynamic-update-slice_fusion.2
  8.8 1.3 dynamic-slice_dynamic-update-slice_fusion.2
  10.8 1.3 dynamic-slice_dynamic-update-slice_fusion.2
  12.8 1.3 dynamic-slice_dynamic-update-slice_fusion.2
  14.8 1.3 dynamic-slice_dynamic-update-slice_fusion.2
  16.8 1.3 dynamic-slice_dynamic-update-slice_fusion.2
  18.9 1.3 dynamic-slice_dynamic-update-slice_fusion.2
  20.9 1.3 dynamic-slice_dynamic-update-slice_fusion.2
  22.9 1.3 dynamic-slice_dynamic-update-slice_fusion.2
  24.9 1.3 dynamic-slice_dynamic-update-slice_fusion.2
  26.9 1.3 dynamic-slice_dynamic-update-slice_fusion.2
  28.9 1.3 dynamic-slice_dynamic-update-slice_fusion.2
  30.9 1.3 dynamic-slice_dynamic-update-slice_fusion.2
  32.9 1.3 dynamic-slice_dynamic-update-slice_fusion.2
  35.0 1.3 dynamic-slice_dynamic-update-slice_fusion.2
  37.0 1.3 dynamic-slice_dynamic-update-slice_fusion.2
  39.0 1.3 dynamic-slice_dynamic-update-slice_fusion.2
  43.0 1.3 dynamic-slice_dynamic-update-slice_fusion.2
  45.0 1.3 dynamic-slice_dynamic-update-slice_fusion.2
  47.0 1.3 dynamic-slice_dynamic-update-slice_fusion.2
  49.0 1.3 dynamic-slice_dynamic-update-slice_fusion.2
  53.1 1.3 dynamic-slice_dynamic-update-slice_fusion.2
  57.1 1.3 dynamic-slice_dynamic-update-slice_fusion.2
  59.1 1.3 dynamic-slice_dynamic-update-slice_fusion.2
  61.1 1.3 dynamic-slice_dynamic-update-slice_fusion.2
  63.1 1.3 dynamic-slice_dynamic-update-slice_fusion.2
  67.1 8.2 %all_gather.12 = bf16[128,3,1024]{2,0,1:T(8,128)(2,1)S(1)} all-gather(bf16[32,3,1024]{2,0,1:T(8,128)(2,1)S(1)} %fusion.12), channel_id=1, replica_groups=mesh['blk'=8,'lag'=4] {'lag'}, dimensions={0}, use_global_device_ids=true | all-gather | bytes 983040 | tf_op jit(solution)/shard_map/all_gather | solution.py:38
  75.6 1.5 collective-permute-start.1
  79.1 33.3 %collective-permute-done.1 = bf16[128,3,1024]{0,2,1:T(8,128)(2,1)} collective-permute-done((bf16[128,3,1024]{0,2,1:T(8,128)(2,1)S(1)}, bf16[128,3,1024]{0,2,1:T(8,128)(2,1)}, u32[]{:S(2)}, u32[]{:S(2)}) %collective-permute-start.1) | collective-permute-done | bytes 786464 | tf_op jit(solution)/shard_map/ppermute | solution.py:23
  112.4 1.4 copy.34
  115.0 103.0 %while.20 = (s32[]{:T(128)}, f32[32,128]{1,0:T(8,128)S(1)}, f32[32,128]{1,0:T(8,128)S(1)}, f32[32,128]{1,0:T(8,128)S(1)}, s32[13]{0:T(128)S(1)}, /*index=5*/bf16...) while((s32[]{:T(128)}, f32[32,128]{1,0:T(8,128)S(1)}, ...), condition=%wide.region_5.6_spmd.clone, body=%wide.region_1.5_spmd.clone.sunk | while | flops 377622560 | bytes 15041106 | solution.py:81
  118.9 1.4 constant_dynamic-slice_fusion.9
  126.8 1.4 constant_dynamic-slice_fusion.9
  134.7 1.4 constant_dynamic-slice_fusion.9
  142.6 1.4 constant_dynamic-slice_fusion.9
  150.6 1.4 constant_dynamic-slice_fusion.9
  158.5 1.4 constant_dynamic-slice_fusion.9
  166.4 1.4 constant_dynamic-slice_fusion.9
  174.3 1.4 constant_dynamic-slice_fusion.9
  182.3 1.4 constant_dynamic-slice_fusion.9
  190.2 1.4 constant_dynamic-slice_fusion.9
  198.1 1.4 constant_dynamic-slice_fusion.9
  206.0 1.4 constant_dynamic-slice_fusion.9
  214.0 1.4 constant_dynamic-slice_fusion.9
  219.3 5.2 %all-gather = f32[4,32,16]{1,2,0:T(8,128)S(1)} all-gather(f32[1,32,16]{1,2,0:T(8,128)S(1)} %multiply_bitcast_fusion), channel_id=1, replica_groups=mesh['blk'=8,'lag'=4] {'lag'}, dimensions={0}, use_global_device_ids=true | all-gather | bytes 10240 | tf_op jit(solution)/shard_map/all_gather | solution.py:46
  226.6 42.9 %all-reduce.3 = (f32[16]{0:T(128)S(1)}, f32[]{:T(128)}) all-reduce(f32[16]{0:T(128)S(1)} %convolution_bitcast_fusion.4, f32[]{:T(128)} %get-tuple-element.209), channel_id=1, replica_groups=mesh['blk'=8,'lag'=4] {'blk','lag'}, use_global_device_ids=true, to_apply=%region_7.8 | all-reduce | flops 17 | bytes 136 | tf_op jit(solution)/shard_map/psum | solution.py:106
  270.7 6.0 %all-reduce.7 = (f32[16,16]{0,1:T(8,128)S(1)}, f32[16]{0:T(128)S(1)}) all-reduce(f32[16,16]{0,1:T(8,128)S(1)} %fusion.69, f32[16]{0:T(128)S(1)} %convolution_bitcast_fusion.3), channel_id=1, replica_groups=mesh['blk'=8,'lag'=4] {'lag'}, use_global_device_ids=true, to_apply=%region_10.11 | all-reduce | flops 272 | bytes 2176 | tf_op jit(solution)/shard_map/psum | solution.py:16
  276.7 16.2 %all-reduce.5 = (f32[16,16]{0,1:T(8,128)S(1)}, f32[16,1]{0,1:T(1,128)S(1)}) all-reduce(f32[16,16]{0,1:T(8,128)S(1)} %get-tuple-element.245, f32[16,1]{0,1:T(1,128)S(1)} %bitcast.228), channel_id=1, replica_groups=mesh['blk'=8,'lag'=4] {'blk'}, use_global_device_ids=true, to_apply=%region_11.12 | all-reduce | flops 272 | bytes 2176 | tf_op jit(solution)/shard_map/psum | solution.py:17
  293.0 1.5 cholesky.59
  297.4 5.2 %all-gather.1 = f32[4,32,16]{1,2,0:T(8,128)S(1)} all-gather(f32[1,32,16]{1,2,0:T(8,128)S(1)} %fusion.6), channel_id=1, replica_groups=mesh['blk'=8,'lag'=4] {'lag'}, dimensions={0}, use_global_device_ids=true | all-gather | bytes 10240 | tf_op jit(solution)/shard_map/all_gather | solution.py:46
  302.7 2.8 collective-permute-start.5
  306.8 3.2 collective-permute-done.4
  310.5 6.0 %all-reduce.6 = (f32[16,16]{0,1:T(8,128)S(1)}, f32[16]{0:T(128)S(1)}) all-reduce(f32[16,16]{0,1:T(8,128)S(1)} %fusion.70, f32[16]{0:T(128)S(1)} %convolution_bitcast_fusion.1), channel_id=1, replica_groups=mesh['blk'=8,'lag'=4] {'lag'}, use_global_device_ids=true, to_apply=%region_16.20 | all-reduce | flops 272 | bytes 2176 | tf_op jit(solution)/shard_map/psum | solution.py:16
  316.6 16.6 %all-reduce.4 = (f32[16,16]{0,1:T(8,128)S(1)}, f32[16,1]{0,1:T(1,128)S(1)}) all-reduce(f32[16,16]{0,1:T(8,128)S(1)} %get-tuple-element.243, f32[16,1]{0,1:T(1,128)S(1)} %bitcast.229), channel_id=1, replica_groups=mesh['blk'=8,'lag'=4] {'blk'}, use_global_device_ids=true, to_apply=%region_17.21 | all-reduce | flops 272 | bytes 2176 | tf_op jit(solution)/shard_map/psum | solution.py:17
  333.3 1.5 cholesky.70
  337.6 5.2 %all-gather.2 = f32[4,32,16]{1,2,0:T(8,128)S(1)} all-gather(f32[1,32,16]{1,2,0:T(8,128)S(1)} %fusion.4), channel_id=1, replica_groups=mesh['blk'=8,'lag'=4] {'lag'}, dimensions={0}, use_global_device_ids=true | all-gather | bytes 10240 | tf_op jit(solution)/shard_map/all_gather | solution.py:46
  342.9 4.7 %collective-permute-start.7 = (f32[16,128]{1,0:T(8,128)S(1)}, f32[16,128]{1,0:T(8,128)S(1)}, u32[]{:S(2)}, u32[]{:S(2)}) collective-permute-start(f32[16,128]{1,0:T(8,128)S(1)} %bitcast.219), channel_id=1, source_target_pairs={{0,28},{4,0},{8,4},{12,8},{16,12},{20,16},{24,20},{28,24},{1,29},{... | collective-permute-start | bytes 24584 | tf_op jit(solution)/shard_map/ppermute | solution.py:23
  349.0 3.2 collective-permute-done.6
  352.5 5.8 %psum.94 = f32[16,16]{0,1:T(8,128)S(1)} all-reduce(f32[16,16]{0,1:T(8,128)S(1)} %fusion.71), channel_id=1, replica_groups=mesh['blk'=8,'lag'=4] {'lag'}, use_global_device_ids=true, to_apply=%region_20.24 | all-reduce | flops 256 | bytes 2048 | tf_op jit(solution)/shard_map/psum | solution.py:16
  358.3 16.5 %psum.95 = f32[16,16]{0,1:T(8,128)S(1)} all-reduce(f32[16,16]{0,1:T(8,128)S(1)} %psum.94), channel_id=1, replica_groups=mesh['blk'=8,'lag'=4] {'blk'}, use_global_device_ids=true, to_apply=%region_21.25 | all-reduce | flops 256 | bytes 2048 | tf_op jit(solution)/shard_map/psum | solution.py:17
  374.9 1.5 cholesky.81
  (421 shorter events, 91.7 us)
Async XLA Ops:
  0.0 0.7 copy-start.2
  75.6 36.8 %collective-permute-start.1 = (bf16[128,3,1024]{0,2,1:T(8,128)(2,1)S(1)}, bf16[128,3,1024]{0,2,1:T(8,128)(2,1)}, u32[]{:S(2)}, u32[]{:S(2)}) collective-permute-start(bf16[128,3,1024]{0,2,1:T(8,128)(2,1)S(1)} %copy.28), channel_id=1, source_target_pairs={{0,28},{4,0},{8,4},{12,8},{16,12},{20,16},{24,20},{28,24},{1,29},{... | collective-permute-start | bytes 2359304 | tf_op jit(solution)/shard_map/ppermute | solution.py:23
  77.1 36.8 %collective-permute-start = (bf16[128,3,1024]{0,2,1:T(8,128)(2,1)S(1)}, bf16[128,3,1024]{0,2,1:T(8,128)(2,1)S(1)}, u32[]{:S(2)}, u32[]{:S(2)}) collective-permute-start(bf16[128,3,1024]{0,2,1:T(8,128)(2,1)S(1)} %copy.28), channel_id=1, source_target_pairs={{0,4},{4,8},{8,12},{12,16},{16,20},{20,24},{24,28},{28,0},{1,5},{5... | collective-permute-start | bytes 2359304 | tf_op jit(solution)/shard_map/ppermute | solution.py:23
  77.9 0.7 copy-start.1
  121.3 1.1 copy-start
  129.2 1.1 copy-start
  137.2 1.1 copy-start
  145.1 1.1 copy-start
  153.0 1.1 copy-start
  160.9 1.1 copy-start
  168.9 1.1 copy-start
  176.8 1.1 copy-start
  184.7 1.1 copy-start
  192.6 1.1 copy-start
  200.6 1.1 copy-start
  208.5 1.1 copy-start
  216.4 1.1 copy-start
  224.6 45.6 %collective-permute-start.3 = (f32[16,128]{1,0:T(8,128)S(1)}, f32[16,128]{1,0:T(8,128)S(1)}, u32[]{:S(2)}, u32[]{:S(2)}) collective-permute-start(f32[16,128]{1,0:T(8,128)S(1)} %bitcast.222), channel_id=1, source_target_pairs={{0,28},{4,0},{8,4},{12,8},{16,12},{20,16},{24,20},{28,24},{1,29},{... | collective-permute-start | bytes 24584 | tf_op jit(solution)/shard_map/ppermute | solution.py:23
  225.4 44.7 %collective-permute-start.2 = (f32[16,128]{1,0:T(8,128)S(1)}, f32[16,128]{1,0:T(8,128)S(1)}, u32[]{:S(2)}, u32[]{:S(2)}) collective-permute-start(f32[16,128]{1,0:T(8,128)S(1)} %bitcast.223), channel_id=1, source_target_pairs={{0,4},{4,8},{8,12},{12,16},{16,20},{20,24},{24,28},{28,0},{1,5},{5... | collective-permute-start | bytes 24584 | tf_op jit(solution)/shard_map/ppermute | solution.py:23
  302.7 4.2 %collective-permute-start.5 = (f32[16,128]{1,0:T(8,128)S(1)}, f32[16,128]{1,0:T(8,128)S(1)}, u32[]{:S(2)}, u32[]{:S(2)}) collective-permute-start(f32[16,128]{1,0:T(8,128)S(1)} %bitcast.225), channel_id=1, source_target_pairs={{0,28},{4,0},{8,4},{12,8},{16,12},{20,16},{24,20},{28,24},{1,29},{... | collective-permute-start | bytes 24584 | tf_op jit(solution)/shard_map/ppermute | solution.py:23
  305.5 4.5 %collective-permute-start.4 = (f32[16,128]{1,0:T(8,128)S(1)}, f32[16,128]{1,0:T(8,128)S(1)}, u32[]{:S(2)}, u32[]{:S(2)}) collective-permute-start(f32[16,128]{1,0:T(8,128)S(1)} %bitcast.226), channel_id=1, source_target_pairs={{0,4},{4,8},{8,12},{12,16},{16,20},{20,24},{24,28},{28,0},{1,5},{5... | collective-permute-start | bytes 24584 | tf_op jit(solution)/shard_map/ppermute | solution.py:23
  342.9 6.1 %collective-permute-start.7 = (f32[16,128]{1,0:T(8,128)S(1)}, f32[16,128]{1,0:T(8,128)S(1)}, u32[]{:S(2)}, u32[]{:S(2)}) collective-permute-start(f32[16,128]{1,0:T(8,128)S(1)} %bitcast.219), channel_id=1, source_target_pairs={{0,28},{4,0},{8,4},{12,8},{16,12},{20,16},{24,20},{28,24},{1,29},{... | collective-permute-start | bytes 24584 | tf_op jit(solution)/shard_map/ppermute | solution.py:23
  347.6 4.5 %collective-permute-start.6 = (f32[16,128]{1,0:T(8,128)S(1)}, f32[16,128]{1,0:T(8,128)S(1)}, u32[]{:S(2)}, u32[]{:S(2)}) collective-permute-start(f32[16,128]{1,0:T(8,128)S(1)} %bitcast.220), channel_id=1, source_target_pairs={{0,4},{4,8},{8,12},{12,16},{16,20},{20,24},{24,28},{28,0},{1,5},{5... | collective-permute-start | bytes 24584 | tf_op jit(solution)/shard_map/ppermute | solution.py:23
